TPU v7x, 32 devices: a whole 2x2x4 slice. The times are simulated.
32 devices in a mesh: groups: 2 (over x), row: 16 (over z, y, core).
Axes of the slice: x: 2, y: 2, z: 4, core: 2. Of those that a mesh axis runs over, the one named last changes fastest.
Arguments:
- basis: float32 [8192, 128], P(('groups', 'row')), parts along dimension 0, may hold values from -6 to 6
- springs: float32 [8192], P(('groups', 'row')), parts along dimension 0, may hold values from 0.25 to 8
- tangent_blocks: float32 [4096, 4096], P(('groups', 'row')), parts along dimension 0, may hold values from -0.375 to 0.375
- tile_rows: int32 [4096], P(('groups', 'row')), parts along dimension 0, may hold values from 0 to 3
- tile_owner: int32 [4096, 1], P(('groups', 'row')), parts along dimension 0, may hold values from 0 to 15, as said below
- tile_offset: int32 [4096], P(('groups', 'row')), parts along dimension 0, may hold values from 0 to 3
- tile_count: int32 [32], P(('groups', 'row')), parts along dimension 0, may hold values from 32 to 128, as said below
Outputs:
- stiff_image: float32 [8192, 128], P(('groups', 'row')), parts along dimension 0
- reduced: float32 [256, 128], P('groups'), parts along dimension 0
There are 2 independent parts, one for each index of `groups`. A program takes and returns all parts, laid end to end along the dimension named above; each array names one. Nothing has to cross between parts.
Inputs may be any that keep to these rules, and one draw needn't show every extreme that they name: The first tile_count[d] slots of device d are live; some device has exactly 128. `tile_owner`: the slab is closed into a shell: every slot of device d names owner (d + o) mod 16 with o one of 0, 1, -1, 4, -4, 5, -5, 8. Among the slots of one device no owner appears more than 32 times, and owner d itself appears exactly 32 times in every device.
All inputs are finite; a program needn't handle non-finite values.
Results may differ from a plain program's by a relative error of at most 0.0003.
Values sent between devices are 32-bit elements; how exact they have to be, the bound alone decides.
A program may use at most 128 MiB of HBM per device.

v0:
```python
import jax
import jax.numpy as jnp
from jax import lax
from jax.sharding import PartitionSpec as P

B = 64
MODES = 128
BR_DEV = 4
CAP = 128


def shards(basis, springs, tangent_blocks, tile_rows, tile_owner, tile_offset, tile_count):
    row_devices = lax.axis_size("row")
    dof_total = basis.shape[0] * row_devices
    own_blocks = basis.reshape(BR_DEV, B, MODES)
    square_blocks = tangent_blocks.reshape(CAP, B, B)
    owner_ids = tile_owner[:, 0]
    gathered = lax.all_gather(own_blocks, "row", axis=0, tiled=True)
    picked = gathered[owner_ids * BR_DEV + tile_offset]
    live_slot = (jnp.arange(CAP, dtype=jnp.int32) < tile_count[0]).astype(jnp.float32)
    row_ids = jnp.arange(BR_DEV, dtype=jnp.int32)
    products = jnp.einsum("sij,sjk->sik", square_blocks, picked, precision=lax.Precision.HIGHEST)
    row_select = (tile_rows[None, :] == row_ids[:, None]).astype(jnp.float32) * live_slot[None, :]
    summed = jnp.dot(row_select, products.reshape(CAP, B * MODES), precision=lax.Precision.HIGHEST)
    stiff_image = springs[:, None] * basis + summed.reshape(BR_DEV * B, MODES)
    partial_term = (
        jnp.einsum("rm,rn->mn", basis, stiff_image, precision=lax.Precision.HIGHEST) / dof_total
    )
    reduced = lax.psum(partial_term, "row")
    return (stiff_image, reduced)


def solution(mesh):
    in_specs = (
        P(("groups", "row"), None),
        P(("groups", "row")),
        P(("groups", "row"), None),
        P(("groups", "row")),
        P(("groups", "row"), None),
        P(("groups", "row")),
        P(("groups", "row")),
    )
    out_specs = (P(("groups", "row"), None), P("groups", None))
    return jax.shard_map(shards, mesh=mesh, in_specs=in_specs, out_specs=out_specs, check_vma=False)
```

profile of v0, /device:TPU:8, one launch (start us, length us, event | category | flops | bytes accessed | tf_op | source)
XLA Modules:
  0.0 163.7 jit_solution(6896301566178183216)
XLA Ops:
  7.2 0.0 all-gather.2.cloned.1.call-start
  7.2 0.7 all-gather.2.cloned.1.call-update
  7.9 0.0 all-reduce.2.cloned.1.call-start
  7.9 1.9 %copy.13 = f32[128,4096]{0,1:T(8,128)S(1)} copy(f32[128,4096]{1,0:T(8,128)} %param.9) | data formatting | bytes 4194304 | tf_op args[2]
  9.9 0.0 copy-start.4
  9.9 0.0 copy-start.5
  9.9 4.5 %copy.14 = f32[128,64,64]{2,1,0:T(8,128)} copy(f32[128,64,64]{0,2,1:T(8,128)S(1)} %bitcast.20) | data formatting | bytes 4194304 | tf_op jit(solution)/shard_map/reshape | solution.py:16
  15.1 0.0 copy-done.4
  15.1 0.0 copy-done.5
  15.1 36.7 %all-gather.2.cloned.1.call-done = f32[64,64,128]{2,1,0:T(8,128)} async-done(((f32[4,64,128]{2,1,0:T(8,128)}), f32[64,64,128]{2,1,0:T(8,128)}) %all-gather.2.cloned.1.call-update) | async-done | bytes 2097168 | tf_op jit(solution)/shard_map/all_gather | solution.py:18
  51.8 4.4 %gather_fusion = f32[128,64,128]{2,1,0:T(8,128)} fusion(f32[64,64,128]{2,1,0:T(8,128)} %all-gather.2.cloned.1.call-done, s32[1024]{0:T(1024)S(1)} %pad_clamp_fusion), kind=kCustom, calls=%fused_computation | custom fusion | bytes 8389120 | tf_op jit(solution)/shard_map/gather | solution.py:19
  56.1 0.0 copy-start.3
  56.1 6.5 %fusion.9 = f32[128,128,64]{1,2,0:T(8,128)S(1)} fusion(f32[128,64,128]{2,1,0:T(8,128)} %gather_fusion, f32[128,64,64]{2,1,0:T(8,128)} %copy.14), kind=kOutput, calls=%fused_computation.17 | convolution fusion | flops 805306368 | bytes 10485760 | tf_op jit(solution)/shard_map/sij,sjk->sik/dot_general | solution.py:22
  62.7 0.0 copy-start
  62.7 0.0 copy-start.2
  62.7 0.0 copy-done.3
  62.7 4.3 %fusion = f32[4,8192]{1,0:T(4,128)S(1)} fusion(f32[16,8,64,128]{3,2,1,0:T(8,128)S(1)} %bitcast.19, f32[128]{0:T(128)S(1)} %compare_convert_fusion, s32[128]{0:T(128)S(1)} %copy-done.3), kind=kOutput, calls=%fused_computation.1 | convolution fusion | flops 50332672 | bytes 4326400 | tf_op jit(solution)/shard_map/dot_general | solution.py:24
  67.1 0.1 reshape.28
  67.2 0.0 copy-done
  67.2 0.0 copy-done.2
  67.2 0.1 multiply_add_fusion
  67.3 0.0 copy-start.1
  67.3 1.0 fusion.3
  68.3 0.0 all-reduce.2.cloned.1.call-update
  68.3 86.9 %all-reduce.2.cloned.1.call-done = f32[128,128]{0,1:T(8,128)} async-done(((f32[128,128]{0,1:T(8,128)}), f32[128,128]{0,1:T(8,128)}) %all-reduce.2.cloned.1.call-update) | async-done | bytes 65552 | tf_op jit(solution)/shard_map/psum | solution.py:29
  155.3 1.6 copy.15
  156.8 0.0 copy-done.1
  (3 shorter events, 0.0 us)
Async XLA Ops:
  7.2 44.6 %all-gather.2.cloned.1.call-start = ((), (), s32[]{:S(2)}) async-start(), calls=%async_computation | async-start | bytes 2228224 | tf_op jit(solution)/shard_map/all_gather | solution.py:18
  7.9 147.4 %all-reduce.2.cloned.1.call-start = ((), (), s32[]{:S(2)}) async-start(), calls=%async_computation.1 | async-start | bytes 131072 | tf_op jit(solution)/shard_map/psum | solution.py:29
  9.9 5.2 %copy-start.4 = (s32[128]{0:T(128)S(1)}, s32[128]{0:T(128)}, u32[]{:S(2)}) copy-start(s32[128]{0:T(128)} %param.12) | copy-start | bytes 1540
  9.9 5.2 %copy-start.5 = (s32[128,1]{0,1:T(1,128)S(1)}, s32[128,1]{0,1:T(1,128)}, u32[]{:S(2)}) copy-start(s32[128,1]{0,1:T(1,128)} %param.11) | copy-start | bytes 1540
  56.1 6.6 %copy-start.3 = (s32[128]{0:T(128)S(1)}, s32[128]{0:T(128)}, u32[]{:S(2)}) copy-start(s32[128]{0:T(128)} %param.10) | copy-start | bytes 1540
  62.7 4.5 %copy-start = (f32[256,128]{1,0:T(8,128)S(1)}, f32[256,128]{1,0:T(8,128)}, u32[]{:S(2)}) copy-start(f32[256,128]{1,0:T(8,128)} %param.7) | copy-start | bytes 393220
  62.7 4.5 %copy-start.2 = (f32[256]{0:T(256)S(1)}, f32[256]{0:T(256)}, u32[]{:S(2)}) copy-start(f32[256]{0:T(256)} %param.8) | copy-start | bytes 3076
  67.3 89.5 %copy-start.1 = (f32[256,128]{1,0:T(8,128)}, f32[256,128]{1,0:T(8,128)S(1)}, u32[]{:S(2)}) copy-start(f32[256,128]{1,0:T(8,128)S(1)} %multiply_add_fusion) | copy-start | bytes 393220
Sparse Core Ops, SparseCore 0:
  10.2 41.5 all-gather.1
  68.5 86.7 all-reduce.1
where the time goes:
time: 164 us
  waiting for transfers between devices  124 us (76%)
  between operations  14.8 us (9%)
  local copies, waits for them, and re-layouts  12.5 us (8%)
  matrix products  11.9 us (7%)
    psum x1, waiting for transfers between devices, shards(): reduced = lax.psum(partial_term, 'row')  86.9 us
    all_gather x1, waiting for transfers between devices, shards(): gathered = lax.all_gather(own_blocks, 'row', axis=0, tiled=True)  36.7 us
    dot_general x1, matrix products, shards(): jnp.einsum('sij,sjk->sik', square_blocks, picked, precision=lax.Precision...  6.52 us
    reshape x1, local copies, waits for them, and re-layouts, shards(): square_blocks = tangent_blocks.reshape(CAP, B, B)  4.52 us
    gather x1, local copies, waits for them, and re-layouts, shards(): picked = gathered[owner_ids * BR_DEV + tile_offset]  4.35 us
    dot_general x1, matrix products, shards(): jnp.dot(row_select, products.reshape(CAP, B * MODES), precision=lax.Preci...  4.34 us
    unnamed x14, local copies, waits for them, and re-layouts  3.52 us
  transfers between devices with their start and end apart: 2, of which 2 were waited for; matrix products, arithmetic and copies ran while one was open for 4% of the time, Pallas kernels for 0%

commit v1 on v0

--- a/solution.py
+++ b/solution.py
@@ -9,13 +9,29 @@
 CAP = 128
 
 
+def gather_around(x, axis, dim):
+    ways, here, step = (lax.axis_size(axis), lax.axis_index(axis), x.shape[dim])
+    lengths = [n * ways if d == dim else n for d, n in enumerate(x.shape)]
+    full = lax.dynamic_update_slice_in_dim(jnp.zeros(lengths, x.dtype), x, here * step, axis=dim)
+    going_up = going_down = x
+    for far in range(1, ways // 2 + 1):
+        going_up = lax.ppermute(going_up, axis, [(d, (d + 1) % ways) for d in range(ways)])
+        full = lax.dynamic_update_slice_in_dim(full, going_up, (here - far) % ways * step, axis=dim)
+        if 2 * far < ways:
+            going_down = lax.ppermute(going_down, axis, [(d, (d - 1) % ways) for d in range(ways)])
+            full = lax.dynamic_update_slice_in_dim(
+                full, going_down, (here + far) % ways * step, axis=dim
+            )
+    return full
+
+
 def shards(basis, springs, tangent_blocks, tile_rows, tile_owner, tile_offset, tile_count):
     row_devices = lax.axis_size("row")
     dof_total = basis.shape[0] * row_devices
     own_blocks = basis.reshape(BR_DEV, B, MODES)
     square_blocks = tangent_blocks.reshape(CAP, B, B)
     owner_ids = tile_owner[:, 0]
-    gathered = lax.all_gather(own_blocks, "row", axis=0, tiled=True)
+    gathered = gather_around(own_blocks, "row", 0)
     picked = gathered[owner_ids * BR_DEV + tile_offset]
     live_slot = (jnp.arange(CAP, dtype=jnp.int32) < tile_count[0]).astype(jnp.float32)
     row_ids = jnp.arange(BR_DEV, dtype=jnp.int32)

time: 164 us -> 179 us (1.091)
  starting transfers between devices: 0.08 us -> 18.6 us
  waiting for transfers between devices: 124 us -> 120 us
    all_gather x1 -> x0, waiting for transfers between devices: 36.7 us -> none  [shards(): gathered = lax.all_gather(own_blocks, 'row', axis=0, tiled=True)]
    ppermute x0 -> x15, waiting for transfers between devices: none -> 21.5 us  [the longest x8 21.5 us: gather_around(): lax.ppermute(going_up, axis, [(d, (d + 1) % ways) for d in range(ways)])]
    ppermute x0 -> x15, starting transfers between devices: none -> 18.6 us  [the longest x7 18.5 us: gather_around(): lax.ppermute(going_down, axis, [(d, (d - 1) % ways) for d in range(ways)])]
    psum x1, waiting for transfers between devices: 86.9 us -> 98.6 us  [shards(): reduced = lax.psum(partial_term, 'row')]
    unnamed x14 -> x10, local copies, waits for them, and re-layouts: 3.52 us -> 4.15 us
  transfers between devices with their start and end apart: 2 -> 16, of which waited for: 2 -> 8; matrix products, arithmetic and copies ran while one was open for 4% -> 4% of each run, Pallas kernels for 0% -> 0%
where the time goes in v1:
time: 179 us
  waiting for transfers between devices  120 us (67%)
  starting transfers between devices  18.6 us (10%)
  between operations  15.2 us (8%)
  local copies, waits for them, and re-layouts  12 us (7%)
  matrix products  11.9 us (7%)
    psum x1, waiting for transfers between devices, shards(): reduced = lax.psum(partial_term, 'row')  98.6 us
    ppermute x8, waiting for transfers between devices, gather_around(): lax.ppermute(going_up, axis, [(d, (d + 1) % ways) for d in range(ways)])  21.5 us
    ppermute x7, starting transfers between devices, gather_around(): lax.ppermute(going_down, axis, [(d, (d - 1) % ways) for d in range(ways)])  18.5 us
    dot_general x1, matrix products, shards(): jnp.einsum('sij,sjk->sik', square_blocks, picked, precision=lax.Precision...  6.52 us
    reshape x1, local copies, waits for them, and re-layouts, shards(): square_blocks = tangent_blocks.reshape(CAP, B, B)  4.54 us
    dot_general x1, matrix products, shards(): jnp.dot(row_select, products.reshape(CAP, B * MODES), precision=lax.Preci...  4.34 us
    unnamed x10, local copies, waits for them, and re-layouts  4.15 us
  transfers between devices with their start and end apart: 16, of which 8 were waited for; matrix products, arithmetic and copies ran while one was open for 4% of the time, Pallas kernels for 0%

profile of v1, /device:TPU:8, one launch (start us, length us, event | category | flops | bytes accessed | tf_op | source)
XLA Modules:
  0.0 178.6 jit_solution(14514599059317237900)
XLA Ops:
  7.2 0.0 all-reduce.2.cloned.1.call-start
  7.2 0.1 collective-permute-start
  7.3 2.6 %collective-permute-start.1 = (f32[4,64,128]{2,1,0:T(8,128)}, f32[4,64,128]{2,1,0:T(8,128)S(1)}, u32[]{:S(2)}, u32[]{:S(2)}) collective-permute-start(f32[4,64,128]{2,1,0:T(8,128)} %bitcast.22), channel_id=1, source_target_pairs={{0,15},{1,0},{2,1},{3,2},{4,3},{5,4},{6,5},{7,6},{8,7},{9,8},{10,9... | collective-permute-start | bytes 393224 | tf_op jit(solution)/shard_map/ppermute | solution.py:21
  9.9 0.7 compare_select_fusion
  11.5 1.9 %copy.10 = f32[128,4096]{0,1:T(8,128)S(1)} copy(f32[128,4096]{1,0:T(8,128)} %param.9) | data formatting | bytes 4194304 | tf_op args[2]
  13.4 4.5 %copy.11 = f32[128,64,64]{2,1,0:T(8,128)} copy(f32[128,64,64]{0,2,1:T(8,128)S(1)} %bitcast.20) | data formatting | bytes 4194304 | tf_op jit(solution)/shard_map/reshape | solution.py:32
  18.0 0.2 broadcast_in_dim.4
  18.2 0.7 copy-done
  18.9 0.0 collective-permute-done
  18.9 0.1 collective-permute-start.2
  19.0 0.0 collective-permute-done.1
  19.0 2.6 %collective-permute-start.3 = (f32[4,64,128]{2,1,0:T(8,128)S(1)}, f32[4,64,128]{2,1,0:T(8,128)S(1)}, u32[]{:S(2)}, u32[]{:S(2)}) collective-permute-start(f32[4,64,128]{2,1,0:T(8,128)S(1)} %collective-permute-done.1), channel_id=1, source_target_pairs={{0,15},{1,0},{2,1},{3,2},{4,3},{5,4},{6,5},{7,6},{8,7},{9,8},{10,9... | collective-permute-start | bytes 393224 | tf_op jit(solution)/shard_map/ppermute | solution.py:21
  21.7 2.7 %collective-permute-done.2 = f32[4,64,128]{2,1,0:T(8,128)S(1)} collective-permute-done((f32[4,64,128]{2,1,0:T(8,128)S(1)}, f32[4,64,128]{2,1,0:T(8,128)S(1)}, u32[]{:S(2)}, u32[]{:S(2)}) %collective-permute-start.2) | collective-permute-done | bytes 131104 | tf_op jit(solution)/shard_map/ppermute | solution.py:18
  24.4 0.0 collective-permute-start.4
  24.4 0.0 collective-permute-done.3
  24.4 2.6 %collective-permute-start.5 = (f32[4,64,128]{2,1,0:T(8,128)S(1)}, f32[4,64,128]{2,1,0:T(8,128)S(1)}, u32[]{:S(2)}, u32[]{:S(2)}) collective-permute-start(f32[4,64,128]{2,1,0:T(8,128)S(1)} %collective-permute-done.3), channel_id=1, source_target_pairs={{0,15},{1,0},{2,1},{3,2},{4,3},{5,4},{6,5},{7,6},{8,7},{9,8},{10,9... | collective-permute-start | bytes 393224 | tf_op jit(solution)/shard_map/ppermute | solution.py:21
  27.1 2.7 %collective-permute-done.4 = f32[4,64,128]{2,1,0:T(8,128)S(1)} collective-permute-done((f32[4,64,128]{2,1,0:T(8,128)S(1)}, f32[4,64,128]{2,1,0:T(8,128)S(1)}, u32[]{:S(2)}, u32[]{:S(2)}) %collective-permute-start.4) | collective-permute-done | bytes 131104 | tf_op jit(solution)/shard_map/ppermute | solution.py:18
  29.8 0.0 collective-permute-start.6
  29.8 0.0 collective-permute-done.5
  29.8 2.6 %collective-permute-start.7 = (f32[4,64,128]{2,1,0:T(8,128)S(1)}, f32[4,64,128]{2,1,0:T(8,128)S(1)}, u32[]{:S(2)}, u32[]{:S(2)}) collective-permute-start(f32[4,64,128]{2,1,0:T(8,128)S(1)} %collective-permute-done.5), channel_id=1, source_target_pairs={{0,15},{1,0},{2,1},{3,2},{4,3},{5,4},{6,5},{7,6},{8,7},{9,8},{10,9... | collective-permute-start | bytes 393224 | tf_op jit(solution)/shard_map/ppermute | solution.py:21
  32.4 2.7 %collective-permute-done.6 = f32[4,64,128]{2,1,0:T(8,128)S(1)} collective-permute-done((f32[4,64,128]{2,1,0:T(8,128)S(1)}, f32[4,64,128]{2,1,0:T(8,128)S(1)}, u32[]{:S(2)}, u32[]{:S(2)}) %collective-permute-start.6) | collective-permute-done | bytes 131104 | tf_op jit(solution)/shard_map/ppermute | solution.py:18
  35.2 0.0 collective-permute-start.8
  35.2 0.0 collective-permute-done.7
  35.2 2.6 %collective-permute-start.9 = (f32[4,64,128]{2,1,0:T(8,128)S(1)}, f32[4,64,128]{2,1,0:T(8,128)S(1)}, u32[]{:S(2)}, u32[]{:S(2)}) collective-permute-start(f32[4,64,128]{2,1,0:T(8,128)S(1)} %collective-permute-done.7), channel_id=1, source_target_pairs={{0,15},{1,0},{2,1},{3,2},{4,3},{5,4},{6,5},{7,6},{8,7},{9,8},{10,9... | collective-permute-start | bytes 393224 | tf_op jit(solution)/shard_map/ppermute | solution.py:21
  37.8 2.7 %collective-permute-done.8 = f32[4,64,128]{2,1,0:T(8,128)S(1)} collective-permute-done((f32[4,64,128]{2,1,0:T(8,128)S(1)}, f32[4,64,128]{2,1,0:T(8,128)S(1)}, u32[]{:S(2)}, u32[]{:S(2)}) %collective-permute-start.8) | collective-permute-done | bytes 131104 | tf_op jit(solution)/shard_map/ppermute | solution.py:18
  40.6 0.0 collective-permute-start.10
  40.6 0.0 collective-permute-done.9
  40.6 2.6 %collective-permute-start.11 = (f32[4,64,128]{2,1,0:T(8,128)S(1)}, f32[4,64,128]{2,1,0:T(8,128)S(1)}, u32[]{:S(2)}, u32[]{:S(2)}) collective-permute-start(f32[4,64,128]{2,1,0:T(8,128)S(1)} %collective-permute-done.9), channel_id=1, source_target_pairs={{0,15},{1,0},{2,1},{3,2},{4,3},{5,4},{6,5},{7,6},{8,7},{9,8},{10,9... | collective-permute-start | bytes 393224 | tf_op jit(solution)/shard_map/ppermute | solution.py:21
  43.2 2.7 %collective-permute-done.10 = f32[4,64,128]{2,1,0:T(8,128)S(1)} collective-permute-done((f32[4,64,128]{2,1,0:T(8,128)S(1)}, f32[4,64,128]{2,1,0:T(8,128)S(1)}, u32[]{:S(2)}, u32[]{:S(2)}) %collective-permute-start.10) | collective-permute-done | bytes 131104 | tf_op jit(solution)/shard_map/ppermute | solution.py:18
  46.0 0.0 collective-permute-start.12
  46.0 0.0 collective-permute-done.11
  46.0 2.6 %collective-permute-start.13 = (f32[4,64,128]{2,1,0:T(8,128)S(1)}, f32[4,64,128]{2,1,0:T(8,128)S(1)}, u32[]{:S(2)}, u32[]{:S(2)}) collective-permute-start(f32[4,64,128]{2,1,0:T(8,128)S(1)} %collective-permute-done.11), channel_id=1, source_target_pairs={{0,15},{1,0},{2,1},{3,2},{4,3},{5,4},{6,5},{7,6},{8,7},{9,8},{10,9... | collective-permute-start | bytes 393224 | tf_op jit(solution)/shard_map/ppermute | solution.py:21
  48.6 2.7 %collective-permute-done.12 = f32[4,64,128]{2,1,0:T(8,128)S(1)} collective-permute-done((f32[4,64,128]{2,1,0:T(8,128)S(1)}, f32[4,64,128]{2,1,0:T(8,128)S(1)}, u32[]{:S(2)}, u32[]{:S(2)}) %collective-permute-start.12) | collective-permute-done | bytes 131104 | tf_op jit(solution)/shard_map/ppermute | solution.py:18
  51.3 0.0 collective-permute-start.14
  51.4 0.0 collective-permute-done.13
  51.4 5.2 %collective-permute-done.14 = f32[4,64,128]{2,1,0:T(8,128)S(1)} collective-permute-done((f32[4,64,128]{2,1,0:T(8,128)S(1)}, f32[4,64,128]{2,1,0:T(8,128)S(1)}, u32[]{:S(2)}, u32[]{:S(2)}) %collective-permute-start.14) | collective-permute-done | bytes 131104 | tf_op jit(solution)/shard_map/ppermute | solution.py:18
  56.7 2.8 %gather_fusion = f32[128,64,128]{2,1,0:T(8,128)} fusion(f32[64,64,128]{2,1,0:T(8,128)S(1)} %constant_dynamic-update-slice_fusion, s32[1024]{0:T(1024)S(1)} %pad_clamp_fusion), kind=kCustom, calls=%fused_computation | custom fusion | bytes 8389120 | tf_op jit(solution)/shard_map/gather | solution.py:35
  59.4 6.5 %fusion.9 = f32[128,128,64]{1,2,0:T(8,128)S(1)} fusion(f32[128,64,128]{2,1,0:T(8,128)} %gather_fusion, f32[128,64,64]{2,1,0:T(8,128)} %copy.11), kind=kOutput, calls=%fused_computation.33 | convolution fusion | flops 805306368 | bytes 10485760 | tf_op jit(solution)/shard_map/sij,sjk->sik/dot_general | solution.py:38
  66.0 0.0 copy-done.3
  66.0 0.0 copy-start.2
  66.0 4.3 %fusion = f32[4,8192]{1,0:T(4,128)S(1)} fusion(f32[16,8,64,128]{3,2,1,0:T(8,128)S(1)} %bitcast.19, f32[128]{0:T(128)S(1)} %compare_convert_fusion, s32[128]{0:T(128)S(1)} %copy-done.3), kind=kOutput, calls=%fused_computation.1 | convolution fusion | flops 50332672 | bytes 4326400 | tf_op jit(solution)/shard_map/dot_general | solution.py:40
  70.3 0.1 reshape.28
  70.4 0.1 multiply_add_fusion
  70.5 0.0 copy-start.1
  70.6 1.0 fusion.3
  71.6 0.0 all-reduce.2.cloned.1.call-update
  71.6 98.6 %all-reduce.2.cloned.1.call-done = f32[128,128]{0,1:T(8,128)} async-done(((f32[128,128]{0,1:T(8,128)}), f32[128,128]{0,1:T(8,128)}) %all-reduce.2.cloned.1.call-update) | async-done | bytes 65552 | tf_op jit(solution)/shard_map/psum | solution.py:45
  170.2 1.6 copy.12
  (22 shorter events, 0.2 us)
Async XLA Ops:
  7.2 163.0 %all-reduce.2.cloned.1.call-start = ((), (), s32[]{:S(2)}) async-start(), calls=%async_computation | async-start | bytes 131072 | tf_op jit(solution)/shard_map/psum | solution.py:45
  7.2 11.7 %collective-permute-start = (f32[4,64,128]{2,1,0:T(8,128)}, f32[4,64,128]{2,1,0:T(8,128)S(1)}, u32[]{:S(2)}, u32[]{:S(2)}) collective-permute-start(f32[4,64,128]{2,1,0:T(8,128)} %bitcast.21), channel_id=1, source_target_pairs={{0,1},{1,2},{2,3},{3,4},{4,5},{5,6},{6,7},{7,8},{8,9},{9,10},{10,1... | collective-permute-start | bytes 393224 | tf_op jit(solution)/shard_map/ppermute | solution.py:18
  7.3 11.7 %collective-permute-start.1 = (f32[4,64,128]{2,1,0:T(8,128)}, f32[4,64,128]{2,1,0:T(8,128)S(1)}, u32[]{:S(2)}, u32[]{:S(2)}) collective-permute-start(f32[4,64,128]{2,1,0:T(8,128)} %bitcast.22), channel_id=1, source_target_pairs={{0,15},{1,0},{2,1},{3,2},{4,3},{5,4},{6,5},{7,6},{8,7},{9,8},{10,9... | collective-permute-start | bytes 393224 | tf_op jit(solution)/shard_map/ppermute | solution.py:21
  18.0 0.9 copy-start
  18.9 5.4 %collective-permute-start.2 = (f32[4,64,128]{2,1,0:T(8,128)S(1)}, f32[4,64,128]{2,1,0:T(8,128)S(1)}, u32[]{:S(2)}, u32[]{:S(2)}) collective-permute-start(f32[4,64,128]{2,1,0:T(8,128)S(1)} %collective-permute-done), channel_id=1, source_target_pairs={{0,1},{1,2},{2,3},{3,4},{4,5},{5,6},{6,7},{7,8},{8,9},{9,10},{10,1... | collective-permute-start | bytes 393224 | tf_op jit(solution)/shard_map/ppermute | solution.py:18
  19.0 5.4 %collective-permute-start.3 = (f32[4,64,128]{2,1,0:T(8,128)S(1)}, f32[4,64,128]{2,1,0:T(8,128)S(1)}, u32[]{:S(2)}, u32[]{:S(2)}) collective-permute-start(f32[4,64,128]{2,1,0:T(8,128)S(1)} %collective-permute-done.1), channel_id=1, source_target_pairs={{0,15},{1,0},{2,1},{3,2},{4,3},{5,4},{6,5},{7,6},{8,7},{9,8},{10,9... | collective-permute-start | bytes 393224 | tf_op jit(solution)/shard_map/ppermute | solution.py:21
  24.4 5.4 %collective-permute-start.4 = (f32[4,64,128]{2,1,0:T(8,128)S(1)}, f32[4,64,128]{2,1,0:T(8,128)S(1)}, u32[]{:S(2)}, u32[]{:S(2)}) collective-permute-start(f32[4,64,128]{2,1,0:T(8,128)S(1)} %collective-permute-done.2), channel_id=1, source_target_pairs={{0,1},{1,2},{2,3},{3,4},{4,5},{5,6},{6,7},{7,8},{8,9},{9,10},{10,1... | collective-permute-start | bytes 393224 | tf_op jit(solution)/shard_map/ppermute | solution.py:18
  24.4 5.4 %collective-permute-start.5 = (f32[4,64,128]{2,1,0:T(8,128)S(1)}, f32[4,64,128]{2,1,0:T(8,128)S(1)}, u32[]{:S(2)}, u32[]{:S(2)}) collective-permute-start(f32[4,64,128]{2,1,0:T(8,128)S(1)} %collective-permute-done.3), channel_id=1, source_target_pairs={{0,15},{1,0},{2,1},{3,2},{4,3},{5,4},{6,5},{7,6},{8,7},{9,8},{10,9... | collective-permute-start | bytes 393224 | tf_op jit(solution)/shard_map/ppermute | solution.py:21
  29.8 5.4 %collective-permute-start.6 = (f32[4,64,128]{2,1,0:T(8,128)S(1)}, f32[4,64,128]{2,1,0:T(8,128)S(1)}, u32[]{:S(2)}, u32[]{:S(2)}) collective-permute-start(f32[4,64,128]{2,1,0:T(8,128)S(1)} %collective-permute-done.4), channel_id=1, source_target_pairs={{0,1},{1,2},{2,3},{3,4},{4,5},{5,6},{6,7},{7,8},{8,9},{9,10},{10,1... | collective-permute-start | bytes 393224 | tf_op jit(solution)/shard_map/ppermute | solution.py:18
  29.8 5.4 %collective-permute-start.7 = (f32[4,64,128]{2,1,0:T(8,128)S(1)}, f32[4,64,128]{2,1,0:T(8,128)S(1)}, u32[]{:S(2)}, u32[]{:S(2)}) collective-permute-start(f32[4,64,128]{2,1,0:T(8,128)S(1)} %collective-permute-done.5), channel_id=1, source_target_pairs={{0,15},{1,0},{2,1},{3,2},{4,3},{5,4},{6,5},{7,6},{8,7},{9,8},{10,9... | collective-permute-start | bytes 393224 | tf_op jit(solution)/shard_map/ppermute | solution.py:21
  35.2 5.4 %collective-permute-start.8 = (f32[4,64,128]{2,1,0:T(8,128)S(1)}, f32[4,64,128]{2,1,0:T(8,128)S(1)}, u32[]{:S(2)}, u32[]{:S(2)}) collective-permute-start(f32[4,64,128]{2,1,0:T(8,128)S(1)} %collective-permute-done.6), channel_id=1, source_target_pairs={{0,1},{1,2},{2,3},{3,4},{4,5},{5,6},{6,7},{7,8},{8,9},{9,10},{10,1... | collective-permute-start | bytes 393224 | tf_op jit(solution)/shard_map/ppermute | solution.py:18
  35.2 5.4 %collective-permute-start.9 = (f32[4,64,128]{2,1,0:T(8,128)S(1)}, f32[4,64,128]{2,1,0:T(8,128)S(1)}, u32[]{:S(2)}, u32[]{:S(2)}) collective-permute-start(f32[4,64,128]{2,1,0:T(8,128)S(1)} %collective-permute-done.7), channel_id=1, source_target_pairs={{0,15},{1,0},{2,1},{3,2},{4,3},{5,4},{6,5},{7,6},{8,7},{9,8},{10,9... | collective-permute-start | bytes 393224 | tf_op jit(solution)/shard_map/ppermute | solution.py:21
  40.6 5.4 %collective-permute-start.10 = (f32[4,64,128]{2,1,0:T(8,128)S(1)}, f32[4,64,128]{2,1,0:T(8,128)S(1)}, u32[]{:S(2)}, u32[]{:S(2)}) collective-permute-start(f32[4,64,128]{2,1,0:T(8,128)S(1)} %collective-permute-done.8), channel_id=1, source_target_pairs={{0,1},{1,2},{2,3},{3,4},{4,5},{5,6},{6,7},{7,8},{8,9},{9,10},{10,1... | collective-permute-start | bytes 393224 | tf_op jit(solution)/shard_map/ppermute | solution.py:18
  40.6 5.4 %collective-permute-start.11 = (f32[4,64,128]{2,1,0:T(8,128)S(1)}, f32[4,64,128]{2,1,0:T(8,128)S(1)}, u32[]{:S(2)}, u32[]{:S(2)}) collective-permute-start(f32[4,64,128]{2,1,0:T(8,128)S(1)} %collective-permute-done.9), channel_id=1, source_target_pairs={{0,15},{1,0},{2,1},{3,2},{4,3},{5,4},{6,5},{7,6},{8,7},{9,8},{10,9... | collective-permute-start | bytes 393224 | tf_op jit(solution)/shard_map/ppermute | solution.py:21
  46.0 5.4 %collective-permute-start.12 = (f32[4,64,128]{2,1,0:T(8,128)S(1)}, f32[4,64,128]{2,1,0:T(8,128)S(1)}, u32[]{:S(2)}, u32[]{:S(2)}) collective-permute-start(f32[4,64,128]{2,1,0:T(8,128)S(1)} %collective-permute-done.10), channel_id=1, source_target_pairs={{0,1},{1,2},{2,3},{3,4},{4,5},{5,6},{6,7},{7,8},{8,9},{9,10},{10,1... | collective-permute-start | bytes 393224 | tf_op jit(solution)/shard_map/ppermute | solution.py:18
  46.0 5.4 %collective-permute-start.13 = (f32[4,64,128]{2,1,0:T(8,128)S(1)}, f32[4,64,128]{2,1,0:T(8,128)S(1)}, u32[]{:S(2)}, u32[]{:S(2)}) collective-permute-start(f32[4,64,128]{2,1,0:T(8,128)S(1)} %collective-permute-done.11), channel_id=1, source_target_pairs={{0,15},{1,0},{2,1},{3,2},{4,3},{5,4},{6,5},{7,6},{8,7},{9,8},{10,9... | collective-permute-start | bytes 393224 | tf_op jit(solution)/shard_map/ppermute | solution.py:21
  51.3 5.3 %collective-permute-start.14 = (f32[4,64,128]{2,1,0:T(8,128)S(1)}, f32[4,64,128]{2,1,0:T(8,128)S(1)}, u32[]{:S(2)}, u32[]{:S(2)}) collective-permute-start(f32[4,64,128]{2,1,0:T(8,128)S(1)} %collective-permute-done.12), channel_id=1, source_target_pairs={{0,1},{1,2},{2,3},{3,4},{4,5},{5,6},{6,7},{7,8},{8,9},{9,10},{10,1... | collective-permute-start | bytes 393224 | tf_op jit(solution)/shard_map/ppermute | solution.py:18
  59.4 6.5 %copy-start.3 = (s32[128]{0:T(128)S(1)}, s32[128]{0:T(128)}, u32[]{:S(2)}) copy-start(s32[128]{0:T(128)} %param.10) | copy-start | bytes 1540
  66.0 4.5 %copy-start.2 = (f32[256]{0:T(256)S(1)}, f32[256]{0:T(256)}, u32[]{:S(2)}) copy-start(f32[256]{0:T(256)} %param.8) | copy-start | bytes 3076
  70.5 101.2 %copy-start.1 = (f32[256,128]{1,0:T(8,128)}, f32[256,128]{1,0:T(8,128)S(1)}, u32[]{:S(2)}) copy-start(f32[256,128]{1,0:T(8,128)S(1)} %multiply_add_fusion) | copy-start | bytes 393220
Sparse Core Ops, SparseCore 0:
  71.7 98.4 all-reduce.1
